TPU v7x, 128 devices: a whole 4x4x4 slice. The times are simulated.
128 devices in a mesh: chan: 32 (over x, z, core), seg: 4 (over y).
Axes of the slice: x: 4, y: 4, z: 4, core: 2. Of those that a mesh axis runs over, the one named last changes fastest.
Arguments:
- traces: bfloat16 [8192, 8, 4096], P('chan', 'seg'), may hold values from -6 to 6
- pairs: int32 [128, 2], P('chan'), may hold values from 0 to 31, as said below
Outputs:
- stacked: float32 [4, 128, 256, 256], P('seg', 'chan')
Inputs may be any that keep to these rules, and one draw needn't show every extreme that they name: `pairs`: the two blocks of a row differ. Row p stands on the device of block h = p // 4. Each block of the row lies within 4 blocks of h, or is the block (h + 16) mod 32, where the cable loops back; in every draw every device has a row with that looped block and a row reaching exactly 4, and block 0 and block 31 both appear.
All inputs are finite; a program needn't handle non-finite values.
Results may differ from a plain program's by a relative error of at most 0.0043.
Values may be sent and summed in bfloat16 or wider, within the bound.
A program may use at most 128 MiB of HBM per device.

v0:
```python
import math

import jax
import jax.numpy as jnp
from jax import lax
from jax.sharding import PartitionSpec as P

NF = 512
FLO = 64
HW = 64
LAGSTEP = 16
NLAG_DEV = 1


def build_tables(length, bins, lowest):
    sample_index = jnp.arange(length, dtype=jnp.int32)
    bin_index = lowest + jnp.arange(bins, dtype=jnp.int32)
    turn_count = sample_index[:, None] * bin_index[None, :] % length
    angles = 2.0 * math.pi / length * turn_count.astype(jnp.float32)
    window_taper = 0.5 - 0.5 * jnp.cos(2.0 * math.pi / length * sample_index.astype(jnp.float32))
    normal_scale = 1.0 / math.sqrt(length)
    cosine = window_taper[:, None] * jnp.cos(angles) * normal_scale
    sine_part = -window_taper[:, None] * jnp.sin(angles) * normal_scale
    dft_table = jnp.concatenate([cosine, sine_part], axis=1).astype(jnp.bfloat16)
    bin_rows = jnp.arange(bins, dtype=jnp.int32)
    in_window = (jnp.abs(bin_rows[:, None] - bin_rows[None, :]) <= HW).astype(jnp.float32)
    counts = jnp.sum(in_window, axis=0)
    matrix = in_window / counts[None, :]
    return (dft_table, matrix)


def whiten(traces_block, dft_table, matrix):
    chan_block, seg_local, length = traces_block.shape
    row_block = traces_block.reshape(chan_block * seg_local, length)
    spectrum = jnp.dot(row_block, dft_table, preferred_element_type=jnp.float32)
    real_part = spectrum[:, :NF]
    imag_part = spectrum[:, NF:]
    power_spec = real_part * real_part + imag_part * imag_part
    smoothed = jnp.dot(power_spec, matrix, precision=lax.Precision.HIGHEST)
    factor = 1.0 / jnp.sqrt(smoothed + 1e-06)
    whitened = jnp.concatenate([real_part * factor, imag_part * factor], axis=1).astype(
        jnp.bfloat16
    )
    return whitened.reshape(chan_block, seg_local, 2 * NF)


def phases(lag_shifts, length):
    bin_index = FLO + jnp.arange(NF, dtype=jnp.int32)
    turn_count = lag_shifts[:, None] * bin_index[None, :] % length
    angles = 2.0 * math.pi / length * turn_count.astype(jnp.float32)
    return (jnp.cos(angles), jnp.sin(angles))


def rotate(spectra, cosine, sine_part):
    shape_out = (cosine.shape[0],) + (1,) * (spectra.ndim - 1) + (NF,)
    cosine = cosine.reshape(shape_out)
    sine_part = sine_part.reshape(shape_out)
    real_part = spectra[..., :NF].astype(jnp.float32)[None]
    imag_part = spectra[..., NF:].astype(jnp.float32)[None]
    real_rot = real_part * cosine - imag_part * sine_part
    imag_rot = real_part * sine_part + imag_part * cosine
    return jnp.concatenate([real_rot, imag_rot], axis=-1).astype(jnp.bfloat16)


def local(traces, pairs):
    chan_block, seg_local, length = traces.shape
    pair_local = pairs.shape[0]
    dft_table, matrix = build_tables(length, NF, FLO)
    whitened = whiten(traces, dft_table, matrix)
    spectra_pool = lax.all_gather(whitened[None], "chan", axis=0, tiled=True)
    first_index = pairs[:, 0]
    second_index = pairs[:, 1]
    first_spec = spectra_pool[first_index]
    second_spec = spectra_pool[second_index].reshape(pair_local, chan_block, -1)
    lag_total = NLAG_DEV * lax.axis_size("seg")
    stack_scale = 1.0 / math.sqrt(NF * seg_local * lax.axis_size("seg"))
    lag_shifts = (
        jnp.arange(NLAG_DEV * lax.axis_size("seg"), dtype=jnp.int32) - lag_total // 2
    ) * LAGSTEP
    cosine, sine_part = phases(lag_shifts, length)
    rotated = rotate(first_spec, cosine, sine_part).reshape(
        NLAG_DEV * lax.axis_size("seg"), pair_local, chan_block, -1
    )
    summed = lax.psum_scatter(
        jnp.einsum("kpix,pjx->kpij", rotated, second_spec, preferred_element_type=jnp.float32),
        "seg",
        scatter_dimension=0,
        tiled=True,
    )
    return summed * stack_scale


def solution(mesh):
    placed = (P("chan", "seg", None), P("chan", None))
    return jax.shard_map(
        local, mesh=mesh, in_specs=placed, out_specs=P("seg", "chan", None, None), check_vma=False
    )
```

profile of v0, /device:TPU:3, one launch (start us, length us, event | category | flops | bytes accessed | tf_op | source)
XLA Modules:
  0.0 381.9 jit_solution(17036607238236821823)
XLA Ops:
  6.7 7.2 %reshape.126 = bf16[512,4096]{1,0:T(8,128)(2,1)} reshape(bf16[256,2,4096]{2,1,0:T(2,128)(2,1)} %param.2) | data formatting | bytes 8388608 | tf_op jit(solution)/shard_map/reshape | solution.py:34
  13.9 35.8 %multiply_convert_fusion.1 = (bf16[4096,512]{1,0:T(8,128)(2,1)S(1)}, bf16[4096,512]{1,0:T(8,128)(2,1)S(1)}) fusion(s32[512]{0:T(512)S(1)} %iota_add_fusion, f32[4096]{0:T(1024)S(1)} %get-tuple-element.17, f32[4096]{0:T(1024)S(1)} %get-tuple-element.18), kind=kLoop, calls=%fused_computation.16 | loop fusion | flops 41943040 | bytes 8423424 | tf_op jit(solution)/shard_map/convert.6
  49.8 4.5 %fusion.10 = f32[512,1024]{1,0:T(8,128)S(1)} fusion(bf16[512,4096]{1,0:T(8,128)(2,1)S(1)} %copy-done, bf16[4096,512]{1,0:T(8,128)(2,1)S(1)} %get-tuple-element.14, bf16[4096,512]{1,0:T(8,128)(2,1)S(1)} %get-tuple-element.13), kind=kOutput, calls=%fused_computation.23 | convolution fusion | flops 4311744512 | bytes 14680064 | tf_op jit(solution)/shard_map/dot_general | solution.py:35
  54.3 2.1 multiply_convert_fusion.3
  56.4 0.2 concatenate.25
  56.7 0.2 concatenate.24
  56.9 1.1 pad_maximum_fusion.1
  58.1 0.2 all-reduce.3.cloned.1.call-start
  58.3 0.2 fusion.26
  58.5 116.4 %all-gather.2.cloned.1.call-done = bf16[32,256,2,1024]{3,1,2,0:T(8,128)(2,1)} async-done(((bf16[1,256,2,1024]{3,1,2,0:T(8,128)(2,1)}), bf16[32,256,2,1024]{3,1,2,0:T(8,128)(2,1)}) %all-gather.2.cloned.1.call-update) | async-done | bytes 33554448 | tf_op jit(solution)/shard_map/all_gather | solution.py:70
  174.9 5.3 %gather_fusion = bf16[4,256,2,1024]{3,1,2,0:T(8,128)(2,1)} fusion(bf16[32,256,2,1024]{3,1,2,0:T(8,128)(2,1)} %all-gather.2.cloned.1.call-done, s32[1024]{0:T(1024)S(1)} %get-tuple-element.20), kind=kCustom, calls=%fused_computation | custom fusion | bytes 8388624 | tf_op jit(solution)/shard_map/gather | solution.py:74
  180.2 6.3 %copy.24 = bf16[4,256,2,1024]{1,3,2,0:T(8,128)(2,1)} copy(bf16[4,256,2,1024]{3,1,2,0:T(8,128)(2,1)} %gather_fusion) | data formatting | bytes 8388608 | tf_op jit(solution)/shard_map/gather | solution.py:74
  186.5 4.9 %gather_fusion.1 = bf16[4,256,2,1024]{3,1,2,0:T(8,128)(2,1)} fusion(bf16[32,256,2,1024]{3,1,2,0:T(8,128)(2,1)} %all-gather.2.cloned.1.call-done, s32[1024]{0:T(1024)S(1)} %get-tuple-element.19), kind=kCustom, calls=%fused_computation.1 | custom fusion | bytes 8388624 | tf_op jit(solution)/shard_map/gather | solution.py:73
  191.4 3.4 slice_convert_fusion.1
  194.8 3.2 copy.26
  198.1 5.2 %copy.25 = f32[4,256,2,512]{3,2,1,0:T(2,128)} copy(f32[4,256,2,512]{3,1,2,0:T(8,128)S(1)} %get-tuple-element.7) | data formatting | bytes 8388608 | tf_op jit(solution)/shard_map/convert_element_type | solution.py:58
  203.3 19.7 %subtract_convert_fusion = (bf16[4,4,256,2,512]{4,3,2,0,1:T(2,128)(2,1)S(1)}, bf16[4,4,256,2,512]{4,3,2,0,1:T(2,128)(2,1)}) fusion(f32[4,512]{1,0:T(4,128)S(1)} %get-tuple-element.12, f32[4,256,2,512]{3,2,1,0:T(2,128)S(1)} %copy.26, f32[4,512]{1,0:T(4,128)S(1)} %get-tuple-element.11, f32[4,256,2,512]{3,2,1,0:T(2,128)} %copy.25), kind=kLoop, calls=%fused_computation.4 | loop fusion | flops 33554432 | bytes 25182208 | tf_op jit(solution)/shard_map/convert
  223.0 18.2 %pad_maximum_fusion = bf16[4,4,256,2,1024]{4,3,2,0,1:T(2,128)(2,1)} fusion(bf16[4,4,256,2,512]{4,3,2,0,1:T(2,128)(2,1)} %get-tuple-element.6, bf16[4,4,256,2,512]{4,3,2,0,1:T(2,128)(2,1)S(1)} %get-tuple-element.5), kind=kLoop, calls=%fused_computation.2 | loop fusion | flops 33554432 | bytes 33554432 | tf_op jit(solution)/shard_map/concatenate | solution.py:62
  241.2 27.6 %convert_element_type.64 = bf16[4,4,256,2048]{3,2,0,1:T(8,128)(2,1)} reshape(bf16[4,4,256,2,1024]{4,3,2,0,1:T(2,128)(2,1)} %pad_maximum_fusion) | data formatting | bytes 33554432 | tf_op jit(solution)/shard_map/convert_element_type | solution.py:62
  268.9 11.3 %convolution_bitcast_fusion = f32[4,4,256,256]{2,3,0,1:T(8,128)} fusion(bf16[4,256,2048,1]{1,2,3,0:T(8,128)(2,1)} %bitcast.27, bf16[4,4,256,2048]{3,2,0,1:T(8,128)(2,1)} %convert_element_type.64), kind=kOutput, calls=%fused_computation.20 | convolution fusion | flops 4294967296 | bytes 25165824 | tf_op jit(solution)/shard_map/kpix,pjx->kpij/dot_general | solution.py:85
  280.1 0.6 dynamic-slice
  280.7 91.0 %all-reduce.3.cloned.1.call-done = f32[4,4,256,256]{2,3,0,1:T(8,128)} async-done(((f32[4,4,256,256]{2,3,0,1:T(8,128)}), f32[4,4,256,256]{2,3,0,1:T(8,128)}) %all-reduce.3.cloned.1.call-update) | async-done | bytes 4194320
  371.7 2.0 dynamic-slice_multiply_fusion
  373.7 1.3 copy.28
  (17 shorter events, 0.4 us)
Async XLA Ops:
  6.5 168.4 %all-gather.2.cloned.1.call-start = ((), (), s32[]{:S(2)}) async-start(), calls=%async_computation | async-start | bytes 34603008 | tf_op jit(solution)/shard_map/all_gather | solution.py:70
  13.9 35.8 %copy-start = (bf16[512,4096]{1,0:T(8,128)(2,1)S(1)}, bf16[512,4096]{1,0:T(8,128)(2,1)}, u32[]{:S(2)}) copy-start(bf16[512,4096]{1,0:T(8,128)(2,1)} %reshape.126) | copy-start | bytes 12582916
  54.3 4.0 %copy-start.1 = (s32[4,2]{0,1:T(2,128)S(1)}, s32[4,2]{0,1:T(2,128)}, u32[]{:S(2)}) copy-start(s32[4,2]{0,1:T(2,128)} %param.3) | copy-start | bytes 100
  58.1 313.7 %all-reduce.3.cloned.1.call-start = ((), (), s32[]{:S(2)}) async-start(), calls=%async_computation.1 | async-start | bytes 8388608
  268.8 11.3 %copy-start.2 = (u32[128]{0:T(128)S(1)}, u32[128]{0:T(128)}, u32[]{:S(2)}) copy-start(u32[128]{0:T(128)} %constant.52) | copy-start | bytes 1540
Sparse Core Ops, SparseCore 0:
  58.2 116.6 all-gather.1
  280.3 91.4 all-reduce.2
where the time goes:
time: 384 us; the launch traced here: 382 us
  waiting for transfers between devices  207 us (54%)
  other arithmetic  80.6 us (21%)
  local copies, waits for them, and re-layouts  62.2 us (16%)
  matrix products  17.8 us (5%)
  between operations  13.5 us (4%)
    all_gather x1, waiting for transfers between devices, local(): spectra_pool = lax.all_gather(whitened[None], 'chan', axis=0, tiled=True)  116 us
    unnamed x3, waiting for transfers between devices  91 us
    another operation x2, other arithmetic  55.6 us
    convert_element_type x1, local copies, waits for them, and re-layouts, rotate(): return jnp.concatenate([real_rot, imag_rot], axis=-1).astype(jnp.bfloat16)  27.6 us
    concatenate x1, other arithmetic, rotate(): return jnp.concatenate([real_rot, imag_rot], axis=-1).astype(jnp.bfloat16)  18.2 us
    gather x2, local copies, waits for them, and re-layouts, local(): second_spec = spectra_pool[second_index].reshape(pair_local, chan_block, -1)  11.6 us
    dot_general x1, matrix products, local(): jnp.einsum('kpix,pjx->kpij', rotated, second_spec, preferred_element_type...  11.3 us
  transfers between devices with their start and end apart: 2, of which 2 were waited for; matrix products, arithmetic and copies ran while one was open for 0% of the time, Pallas kernels for 0%

commit v1 on v0

v1 whole, which is shorter than its diff:
```python
import math

import jax
import jax.numpy as jnp
import numpy as np
from jax import lax
from jax.experimental import pallas as pl
from jax.experimental.pallas import tpu as pltpu
from jax.sharding import PartitionSpec as P

CB = 256
L = 4096
NF = 512
FLO = 64
HW = 64
LAGSTEP = 16
NLAG = 4
PAIRS = 4
BLOCKS = 32
SEG = 2
CHUNK = 64
CHUNKS = CB // CHUNK
GROUPS = ((0, 1), (2,), (3,))
TABLE_CUTS = 4
MESH = pl.DeviceIdType.MESH
BF16 = jnp.bfloat16
F32 = jnp.float32

ZP, ZM, ZA, ZB, ZC, XN, XE, ZE, LA, LB, SB = 0, 2, 4, 5, 6, 7, 9, 10, 11, 15, 19
COPIES = 25


def host_tables():
    sample = np.arange(L)
    bins = FLO + np.arange(NF)
    angles = 2.0 * np.pi / L * ((sample[:, None] * bins[None, :]) % L)
    taper = (0.5 - 0.5 * np.cos(2.0 * np.pi / L * sample))[:, None] / math.sqrt(L)
    table = np.concatenate([taper * np.cos(angles), -taper * np.sin(angles)], axis=1)
    rows = np.arange(NF)
    window = np.abs(rows[:, None] - rows[None, :]) <= HW
    phase = 2.0 * np.pi / L * ((LAGSTEP * bins) % L)
    small = np.zeros((8, NF), np.float32)
    small[0], small[1] = np.cos(phase), np.sin(phase)
    small[2], small[3] = np.cos(2.0 * phase), np.sin(2.0 * phase)
    small[4] = 1.0 / window.sum(axis=0)
    return table.astype(BF16), window.astype(BF16), small


def regions(group):
    new = len(group) * CHUNK
    old = group[0] * CHUNK
    shapes = [(new, -(-(old + new) // 128) * 128)]
    if old:
        shapes.append((new, -(-old // 128) * 128))
    return new, old, shapes


def kernel(traces, table_hbm, window, small, pairs, out, *scratch):
    pools = scratch[:CHUNKS]
    scratch = scratch[CHUNKS:]
    spans = [len(regions(group)[2]) for group in GROUPS]
    sends, lands = [], []
    for span in spans:
        sends.append(scratch[:span])
        lands.append(scratch[span : 2 * span])
        scratch = scratch[2 * span :]
    rows_in, table, white, rot, in_sem, ssem, rsem, ysem, yrsem = scratch

    h = lax.axis_index("chan")
    y = lax.axis_index("seg")
    core = h % 2
    z = (h // 2) % 4
    x = h // 8
    away = 1 - 2 * (z // 2)
    outer = (z == 0) | (z == 3)
    gives = (x + away >= 0) & (x + away <= 3)
    takes = (x - away >= 0) & (x - away <= 3)

    def node(xx, zz, cc=None):
        return ((xx % 4) * 8 + (zz % 4) * 2 + (core if cc is None else cc), y)

    def slot(xx, zz, cc=None):
        return node(xx, zz, cc)[0]

    sibling = node(x, z, 1 - core)
    partners = [node(x, z + 1), node(x, z + 3), node(x + 1, z), node(x + 3, z), sibling]
    partners += [(h, (y + d) % 4) for d in (1, 2, 3)]

    fetch_rows = [
        pltpu.make_async_copy(
            traces.at[pl.ds(t * CHUNK, CHUNK)], rows_in.at[pl.ds(t * CHUNK, CHUNK)], in_sem.at[t]
        )
        for t in range(CHUNKS)
    ]
    cut = L // TABLE_CUTS
    fetch_table = [
        pltpu.make_async_copy(
            table_hbm.at[pl.ds(i * cut, cut)], table.at[pl.ds(i * cut, cut)], in_sem.at[CHUNKS + i]
        )
        for i in range(TABLE_CUTS)
    ]
    fetch_rows[0].start()
    for copy in fetch_table:
        copy.start()
    for copy in fetch_rows[1:]:
        copy.start()

    barrier = pltpu.get_barrier_semaphore()
    for partner in partners:
        pl.semaphore_signal(barrier, inc=1, device_id=partner, device_id_type=MESH)

    def spectra(t):
        fetch_rows[t].wait()
        rows = rows_in[t * CHUNK : (t + 1) * CHUNK].reshape(SEG * CHUNK, L)
        if t == 0:
            spec = jnp.zeros((SEG * CHUNK, 2 * NF), F32)
            for i in range(TABLE_CUTS):
                fetch_table[i].wait()
                spec += jnp.dot(
                    rows[:, i * cut : (i + 1) * cut],
                    table[i * cut : (i + 1) * cut],
                    preferred_element_type=F32,
                )
        else:
            spec = jnp.dot(rows, table[...], preferred_element_type=F32)
        real, imag = spec[:, :NF], spec[:, NF:]
        power = real * real + imag * imag
        high = power.astype(BF16)
        low = (power - high.astype(F32)).astype(BF16)
        smooth = jnp.dot(high, window[...], preferred_element_type=F32)
        smooth += jnp.dot(low, window[...], preferred_element_type=F32)
        factor = lax.rsqrt(smooth * small[4:5, :] + 1e-06)
        for j in range(2 * NF // 128):
            part = real if j * 128 < NF else imag
            lanes = slice(j * 128 % NF, j * 128 % NF + 128)
            white[j] = part[:, lanes] * factor[:, lanes]
            for s in range(SEG):
                rows = white[j, pl.ds(s, CHUNK, stride=SEG), :]
                pools[t][h, s, :, j * 128 : (j + 1) * 128] = rows.astype(BF16)

    started = []

    def remote(t, what, block, part, target):
        view = pools[t].at[(block, *part)]
        return pltpu.make_async_remote_copy(
            src_ref=view,
            dst_ref=view,
            send_sem=ssem.at[t, what],
            recv_sem=rsem.at[t, what],
            device_id=target,
            device_id_type=MESH,
        )

    def on(condition, act):
        if condition is None:
            act()
        else:
            pl.when(condition)(act)

    def send(t, what, block, part, target, condition=None):
        on(condition, lambda: remote(t, what, block, part, target).start())
        started.append(
            lambda: on(condition, lambda: remote(t, what, block, part, target).wait_send())
        )

    def take(t, what, block, part, condition=None):
        on(condition, lambda: remote(t, what, block, part, sibling).wait_recv())

    quarter = CHUNK // 4
    loop_parts = [
        (0,),
        (1, pl.ds(2 * quarter, 2 * quarter)),
        (1, pl.ds(quarter, quarter)),
        (1, pl.ds(0, quarter)),
    ]
    middle = jnp.where(outer, 1, -1)
    loop_way = [-away, -away, -away * middle, away]

    def first_hop(t):
        own = slot(x, z)
        send(t, ZP, own, (0,), node(x, z + 1))
        send(t, ZM + 1, own, (1,), node(x, z + 3))
        send(t, ZP + 1, own, (1,), node(x, z + 1), z != 3)
        send(t, ZM, own, (0,), node(x, z + 3), z != 0)
        for i, part in enumerate(loop_parts):
            send(t, LA + i, own, part, node(x + loop_way[i] + 4, z))
        send(t, SB, own, (), sibling)

    def second_hop(t):
        below, above = slot(x, z + 3), slot(x, z + 1)
        take(t, ZP, below, (0,))
        send(t, ZA, below, (0,), node(x, z + 1), z != 2)
        take(t, ZM + 1, above, (1,))
        send(t, ZB, above, (1,), node(x, z + 3), z != 1)
        take(t, ZP + 1, below, (1,), z != 0)
        take(t, ZM, above, (0,), z != 3)
        side = z // 3
        send(
            t,
            ZC,
            slot(x, z + 1 + 2 * side),
            (side,),
            node(x, z + 3 + 2 * side),
            outer,
        )
        send(t, XE, slot(x, 3 - z), (side,), node(x + away + 4, z), outer & gives)
        send(t, SB + 1, below, (), sibling, z != 0)
        send(t, SB + 2, above, (), sibling, z != 3)

    def loop_hop(t):
        for i, part in enumerate(loop_parts):
            block = slot(x - loop_way[i] + 4, z)
            take(t, LA + i, block, part)
            send(t, LB + i, block, part, node(x + loop_way[i] + 4, z))

    def cross(t):
        far = slot(x, z + 2)
        side = z // 3
        on(z != 3, lambda: remote(t, ZA, far, (0,), sibling).wait_recv())
        on(z != 0, lambda: remote(t, ZB, far, (1,), sibling).wait_recv())
        on(outer, lambda: remote(t, ZC, far, (1 - side,), sibling).wait_recv())
        for s in range(SEG):
            send(t, XN + s, far, (s,), node(x + away + 4, z), gives)
        send(t, SB + 3, far, (), sibling, core == z // 2)

    def crossed(t):
        near = slot(x - away + 4, z + 2)
        for s in range(SEG):
            take(t, XN + s, near, (s,), takes)
        inner = jnp.logical_not(outer)
        send(t, ZE, near, (jnp.clip(2 - z, 0, 1),), node(x, 3 * (z // 2)), inner & takes)
        send(t, SB + 4, near, (), sibling, takes & (core == 1 - z // 2))

    def last_hop(t):
        edge = slot(x - away + 4, 3 - z)
        side = z // 3
        take(t, XE, edge, (side,), outer & takes)
        take(t, ZE, edge, (1 - side,), outer & takes)
        send(t, SB + 5, edge, (), sibling, outer & takes)

    def settle(t):
        other = 1 - core
        for i in range(len(loop_parts)):
            take(t, LB + i, slot(x + 2, z), loop_parts[i])
        take(t, SB, slot(x, z, other), ())
        take(t, SB + 1, slot(x, z + 3, other), (), z != 0)
        take(t, SB + 2, slot(x, z + 1, other), (), z != 3)
        take(t, SB + 3, slot(x, z + 2, other), (), other == z // 2)
        take(t, SB + 4, slot(x - away + 4, z + 2, other), (), takes & (other == 1 - z // 2))
        take(t, SB + 5, slot(x - away + 4, 3 - z, other), (), outer & takes)

    def rotate(block, sign):
        real, imag = block[:, :NF].astype(F32), block[:, NF:].astype(F32)
        cos1, sin1 = small[0:1, :], small[1:2, :] * sign
        cos2, sin2 = small[2:3, :], small[3:4, :] * sign
        rc, ic, rs, js = real * cos1, imag * cos1, real * sin1, imag * sin1
        back2 = (real * cos2 + imag * sin2, imag * cos2 - real * sin2)
        back1 = (rc + js, ic - rs)
        ahead = (rc - js, ic + rs)
        return back2, back1, None, ahead

    def gather_rows(block, s, chunks):
        parts = [pools[t][block, s] for t in chunks]
        return parts[0] if len(parts) == 1 else jnp.concatenate(parts, axis=0)

    def correlate(g):
        group = GROUPS[g]
        new, old, shapes = regions(group)
        earlier = tuple(range(group[0]))

        def product(first, second, chunks, sign):
            total = None
            for s in range(SEG):
                for i, t in enumerate(group):
                    block = pools[t][first, s]
                    for m, turned in enumerate(rotate(block, sign)):
                        at = m * new + i * CHUNK
                        if turned is None:
                            rot[s, at : at + CHUNK] = block
                        else:
                            rot[s, at : at + CHUNK, :NF] = turned[0].astype(BF16)
                            rot[s, at : at + CHUNK, NF:] = turned[1].astype(BF16)
                term = lax.dot_general(
                    rot[s, : NLAG * new],
                    gather_rows(second, s, chunks),
                    (((1,), (1,)), ((), ())),
                    preferred_element_type=F32,
                )
                total = term if total is None else total + term
            return total

        def one_pair(p, carry):
            first, second = pairs[p, 0], pairs[p, 1]
            todo = [(first, second, earlier + group, 1.0)]
            if old:
                todo.append((second, first, earlier, -1.0))
            for r, (a, b, chunks, sign) in enumerate(todo):
                total = product(a, b, chunks, sign)
                wide = total.shape[1]
                for m in range(NLAG):
                    sends[g][r][m, p, :, :wide] = total[m * new : (m + 1) * new].astype(BF16)
                    if wide < shapes[r][1]:
                        sends[g][r][m, p, :, wide:] = jnp.zeros((new, shapes[r][1] - wide), BF16)
                for d in (2, 1, 3):
                    across(g, r, d, p).start()
            return carry

        lax.fori_loop(0, PAIRS, one_pair, 0)

    def across(g, r, d, p):
        place = sum(spans[:g]) + r
        lag = (y + d) % 4
        return pltpu.make_async_remote_copy(
            src_ref=sends[g][r].at[lag, p],
            dst_ref=lands[g][r].at[d - 1, p],
            send_sem=ysem.at[place, d - 1, p],
            recv_sem=yrsem.at[place, d - 1, p],
            device_id=(h, lag),
            device_id_type=MESH,
        )

    def finish(g):
        new, old, shapes = regions(GROUPS[g])
        scale = 1.0 / math.sqrt(NF * SEG * 4)

        def one_pair(p, carry):
            for r in range(len(shapes)):
                total = sends[g][r][y, p].astype(F32)
                for d in (1, 2, 3):
                    across(g, r, d, p).wait_recv()
                    total += lands[g][r][d - 1, p].astype(F32)
                total *= scale
                if r == 0:
                    out[0, p, old : old + new, : old + new] = total[:, : old + new]
                else:
                    out[0, p, :old, old : old + new] = total.T[:old]
            return carry

        lax.fori_loop(0, PAIRS, one_pair, 0)

    spectra(0)
    pl.semaphore_wait(barrier, len(partners))
    first_hop(0)
    spectra(1)
    first_hop(1)
    spectra(2)
    spectra(3)
    second_hop(0)
    loop_hop(0)
    first_hop(2)
    cross(0)
    second_hop(1)
    loop_hop(1)
    first_hop(3)
    cross(1)
    crossed(0)
    second_hop(2)
    loop_hop(2)
    last_hop(0)
    settle(0)
    cross(2)
    crossed(1)
    second_hop(3)
    loop_hop(3)
    last_hop(1)
    settle(1)
    cross(3)
    correlate(0)
    crossed(2)
    last_hop(2)
    settle(2)
    crossed(3)
    correlate(1)
    last_hop(3)
    settle(3)
    correlate(2)
    for g in range(len(GROUPS)):
        finish(g)
    for done in started:
        done()

    def sent(p, carry):
        for g in range(len(GROUPS)):
            for r in range(spans[g]):
                for d in (1, 2, 3):
                    across(g, r, d, p).wait_send()
        return carry

    lax.fori_loop(0, PAIRS, sent, 0)


def local(traces, pairs):
    table, window, small = host_tables()
    scratch = [pltpu.VMEM((BLOCKS, SEG, CHUNK, 2 * NF), BF16) for _ in range(CHUNKS)]
    spans = 0
    for group in GROUPS:
        shapes = regions(group)[2]
        spans += len(shapes)
        scratch += [pltpu.VMEM((NLAG, PAIRS, *shape), BF16) for shape in shapes]
        scratch += [pltpu.VMEM((3, PAIRS, *shape), BF16) for shape in shapes]
    widest = max(len(group) for group in GROUPS) * CHUNK
    scratch += [
        pltpu.VMEM((CB, SEG, L), BF16),
        pltpu.VMEM((L, 2 * NF), BF16),
        pltpu.VMEM((2 * NF // 128, SEG * CHUNK, 128), F32),
        pltpu.VMEM((SEG, NLAG * widest, 2 * NF), BF16),
        pltpu.SemaphoreType.DMA((CHUNKS + TABLE_CUTS,)),
        pltpu.SemaphoreType.DMA((CHUNKS, COPIES)),
        pltpu.SemaphoreType.DMA((CHUNKS, COPIES)),
        pltpu.SemaphoreType.DMA((spans, 3, PAIRS)),
        pltpu.SemaphoreType.DMA((spans, 3, PAIRS)),
    ]
    return pl.pallas_call(
        kernel,
        out_shape=jax.ShapeDtypeStruct((1, PAIRS, CB, CB), F32),
        in_specs=[
            pl.BlockSpec(memory_space=pl.ANY),
            pl.BlockSpec(memory_space=pl.ANY),
            pl.BlockSpec(memory_space=pltpu.VMEM),
            pl.BlockSpec(memory_space=pltpu.VMEM),
            pl.BlockSpec(memory_space=pltpu.SMEM),
        ],
        out_specs=pl.BlockSpec(memory_space=pltpu.VMEM),
        scratch_shapes=scratch,
        compiler_params=pltpu.CompilerParams(
            collective_id=0, has_side_effects=True, vmem_limit_bytes=62 << 20
        ),
        name="correlate_pairs",
    )(traces, jnp.asarray(table), jnp.asarray(window), jnp.asarray(small), pairs)


def solution(mesh):
    placed = (P("chan", "seg", None), P("chan", None))
    return jax.shard_map(
        local, mesh=mesh, in_specs=placed, out_specs=P("seg", "chan", None, None), check_vma=False
    )
```

time: 384 us -> 88.3 us (0.23)
  waiting for transfers between devices: 207 us -> 0 us
  Pallas kernels: 0 us -> 84.2 us
  other arithmetic: 80.6 us -> 0 us
  local copies, waits for them, and re-layouts: 62.2 us -> 3.62 us
  matrix products: 17.8 us -> 0 us
  between operations: 13.5 us -> 0.01 us
    all_gather x1 -> x0, waiting for transfers between devices: 116 us -> none  [local(): spectra_pool = lax.all_gather(whitened[None], 'chan', axis=0, tiled=True)]
    unnamed x3 -> x0, waiting for transfers between devices: 91 us -> none
    pallas_call x0 -> x1, Pallas kernels: none -> 84.2 us  [local(): pl.pallas_call(kernel, out_shape=jax.ShapeDtypeStruct((1, PAIRS, CB, CB),...]
    another operation x2 -> x0, other arithmetic: 55.6 us -> none
    convert_element_type x3 -> x0, local copies, waits for them, and re-layouts: 36.1 us -> none  [the longest x1 27.6 us: rotate(): return jnp.concatenate([real_rot, imag_rot], axis=-1).astype(jnp.bfloat16)]
    concatenate x2 -> x0, other arithmetic: 19.3 us -> none  [the longest x1 18.2 us: rotate(): return jnp.concatenate([real_rot, imag_rot], axis=-1).astype(jnp.bfloat16)]
    dot_general x3 -> x0, matrix products: 17.8 us -> none  [the longest x1 11.3 us: local(): jnp.einsum('kpix,pjx->kpij', rotated, second_spec, preferred_element_type...]
    gather x3 -> x0, local copies, waits for them, and re-layouts: 16.5 us -> none  [the longest x2 11.6 us: local(): second_spec = spectra_pool[second_index].reshape(pair_local, chan_block, -1)]
  transfers between devices with their start and end apart: 2 -> 0, of which waited for: 2 -> 0; matrix products, arithmetic and copies ran while one was open for 0% -> 0% of each run, Pallas kernels for 0% -> 0%
where the time goes in v1:
time: 88.3 us; the launch traced here: 87.8 us
  Pallas kernels  84.2 us (95%)
  local copies, waits for them, and re-layouts  3.62 us (4%)
    pallas_call x1, Pallas kernels, local(): pl.pallas_call(kernel, out_shape=jax.ShapeDtypeStruct((1, PAIRS, CB, CB),...  84.2 us
    unnamed x2, local copies, waits for them, and re-layouts  3.62 us

profile of v1, /device:TPU:3, one launch (start us, length us, event | category | flops | bytes accessed | tf_op | source)
XLA Modules:
  0.0 87.8 jit_solution(13607475369598165257)
XLA Ops:
  0.0 1.3 %copy.6.pairs = s32[4,2]{1,0:T(4,128)} copy(s32[4,2]{0,1:T(2,128)} %param.6) | data formatting | bytes 64 | tf_op args[1]
  1.3 84.2 %correlate_pairs.1 = f32[1,4,256,256]{3,2,1,0:T(8,128)} custom-call(bf16[256,2,4096]{2,1,0:T(2,128)(2,1)} %traces.1, bf16[4096,1024]{1,0:T(8,128)(2,1)} %constant.6.clone.table_hbm, bf16[512,512]{1,0:T(8,128)(2,1)} %constant.7.clone.window, f32[8,512]{1,0:T(8,128)} %constant.8.clone.small, s32[4,2]{1,0:T(4,128)} %copy.6.pairs), custom_call_target="tpu_custom_call" | custom-call | tf_op jit(solution)/shard_map/correlate_pairs/pallas_call | solution.py:413
  85.6 2.3 %copy.8 = f32[1,4,256,256]{3,2,1,0:T(8,128)} copy(f32[1,4,256,256]{3,2,1,0:T(8,128)} %correlate_pairs.1) | data formatting | bytes 2097152

commit v2 on v1

--- a/solution.py
+++ b/solution.py
@@ -18,13 +18,25 @@
 PAIRS = 4
 BLOCKS = 32
 SEG = 2
-CHUNK = 64
-CHUNKS = CB // CHUNK
+SIZES = (64, 64, 64, 64)
+CHUNKS = len(SIZES)
+STARTS = tuple(sum(SIZES[:t]) for t in range(CHUNKS))
 GROUPS = ((0, 1), (2,), (3,))
-TABLE_CUTS = 4
+TABLE_CUTS = 8
+AHEAD = 7
 MESH = pl.DeviceIdType.MESH
 BF16 = jnp.bfloat16
 F32 = jnp.float32
+
+ORDER = (
+    "S0", "Z0", "O0", "S1", "S2", "S3", "Z1", "O2", "O1", "O3", "B1", "M0", "B0", "H0", "I0",
+    "M2", "H1", "I1", "X0", "L0", "Z2", "X1", "C0", "B3", "H2", "B2", "I2", "L1", "Z3", "E0",
+    "T0", "M1", "X2", "C1", "H3", "L2", "I3", "E1", "T1", "K00", "K01", "K02", "K03", "X3", "C2",
+    "L3", "E2", "T2", "K10", "K11", "K12", "K13", "M3", "C3", "E3", "T3", "K20", "K21", "K22",
+    "K23", "G0", "G1", "G2",
+)
+
+LAST = "K" + str(len(GROUPS) - 1) + str(PAIRS - 1)
 
 ZP, ZM, ZA, ZB, ZC, XN, XE, ZE, LA, LB, SB = 0, 2, 4, 5, 6, 7, 9, 10, 11, 15, 19
 COPIES = 25
@@ -47,15 +59,15 @@
 
 
 def regions(group):
-    new = len(group) * CHUNK
-    old = group[0] * CHUNK
+    new = sum(SIZES[t] for t in group)
+    old = STARTS[group[0]]
     shapes = [(new, -(-(old + new) // 128) * 128)]
     if old:
         shapes.append((new, -(-old // 128) * 128))
     return new, old, shapes
 
 
-def kernel(traces, table_hbm, window, small, pairs, out, *scratch):
+def kernel(traces, table_hbm, window_hbm, small_hbm, pairs, result, *scratch):
     pools = scratch[:CHUNKS]
     scratch = scratch[CHUNKS:]
     spans = [len(regions(group)[2]) for group in GROUPS]
@@ -64,7 +76,7 @@
         sends.append(scratch[:span])
         lands.append(scratch[span : 2 * span])
         scratch = scratch[2 * span :]
-    rows_in, table, white, rot, in_sem, ssem, rsem, ysem, yrsem = scratch
+    rows_in, table, window, small, white, rot, out, in_sem, ssem, rsem, ysem, yrsem = scratch
 
     h = lax.axis_index("chan")
     y = lax.axis_index("seg")
@@ -88,7 +100,9 @@
 
     fetch_rows = [
         pltpu.make_async_copy(
-            traces.at[pl.ds(t * CHUNK, CHUNK)], rows_in.at[pl.ds(t * CHUNK, CHUNK)], in_sem.at[t]
+            traces.at[pl.ds(STARTS[t], SIZES[t])],
+            rows_in.at[pl.ds(STARTS[t], SIZES[t])],
+            in_sem.at[t],
         )
         for t in range(CHUNKS)
     ]
@@ -99,10 +113,12 @@
         )
         for i in range(TABLE_CUTS)
     ]
-    fetch_rows[0].start()
-    for copy in fetch_table:
-        copy.start()
-    for copy in fetch_rows[1:]:
+    fetch_small = [
+        pltpu.make_async_copy(window_hbm, window, in_sem.at[CHUNKS + TABLE_CUTS]),
+        pltpu.make_async_copy(small_hbm, small, in_sem.at[CHUNKS + TABLE_CUTS + 1]),
+    ]
+    fetches = [fetch_rows[0], *fetch_table, *fetch_small, *fetch_rows[1:]]
+    for copy in fetches[:AHEAD]:
         copy.start()
 
     barrier = pltpu.get_barrier_semaphore()
@@ -111,11 +127,14 @@
 
     def spectra(t):
         fetch_rows[t].wait()
-        rows = rows_in[t * CHUNK : (t + 1) * CHUNK].reshape(SEG * CHUNK, L)
+        size = SIZES[t]
+        rows = rows_in[STARTS[t] : STARTS[t] + size].reshape(SEG * size, L)
         if t == 0:
-            spec = jnp.zeros((SEG * CHUNK, 2 * NF), F32)
+            spec = jnp.zeros((SEG * size, 2 * NF), F32)
             for i in range(TABLE_CUTS):
                 fetch_table[i].wait()
+                for copy in fetches[i + AHEAD : i + AHEAD + 1]:
+                    copy.start()
                 spec += jnp.dot(
                     rows[:, i * cut : (i + 1) * cut],
                     table[i * cut : (i + 1) * cut],
@@ -123,6 +142,9 @@
                 )
         else:
             spec = jnp.dot(rows, table[...], preferred_element_type=F32)
+        if t == 0:
+            for copy in fetch_small:
+                copy.wait()
         real, imag = spec[:, :NF], spec[:, NF:]
         power = real * real + imag * imag
         high = power.astype(BF16)
@@ -133,9 +155,9 @@
         for j in range(2 * NF // 128):
             part = real if j * 128 < NF else imag
             lanes = slice(j * 128 % NF, j * 128 % NF + 128)
-            white[j] = part[:, lanes] * factor[:, lanes]
+            white[j, : SEG * size] = part[:, lanes] * factor[:, lanes]
             for s in range(SEG):
-                rows = white[j, pl.ds(s, CHUNK, stride=SEG), :]
+                rows = white[j, pl.ds(s, size, stride=SEG), :]
                 pools[t][h, s, :, j * 128 : (j + 1) * 128] = rows.astype(BF16)
 
     started = []
@@ -166,52 +188,55 @@
     def take(t, what, block, part, condition=None):
         on(condition, lambda: remote(t, what, block, part, sibling).wait_recv())
 
-    quarter = CHUNK // 4
-    loop_parts = [
-        (0,),
-        (1, pl.ds(2 * quarter, 2 * quarter)),
-        (1, pl.ds(quarter, quarter)),
-        (1, pl.ds(0, quarter)),
-    ]
+    def loop_parts(t):
+        size = SIZES[t]
+        low = max(size // 4, 16)
+        cuts = [(0,), (1, pl.ds(size // 2, size // 2))]
+        if low < size // 2:
+            cuts.append((1, pl.ds(low, size // 2 - low)))
+        cuts.append((1, pl.ds(0, low)))
+        return list(zip(cuts, loop_way))
+
     middle = jnp.where(outer, 1, -1)
     loop_way = [-away, -away, -away * middle, away]
 
-    def first_hop(t):
+    def ring(t):
         own = slot(x, z)
         send(t, ZP, own, (0,), node(x, z + 1))
         send(t, ZM + 1, own, (1,), node(x, z + 3))
         send(t, ZP + 1, own, (1,), node(x, z + 1), z != 3)
         send(t, ZM, own, (0,), node(x, z + 3), z != 0)
-        for i, part in enumerate(loop_parts):
-            send(t, LA + i, own, part, node(x + loop_way[i] + 4, z))
-        send(t, SB, own, (), sibling)
-
-    def second_hop(t):
+
+    def loop(t):
+        for i, (part, way) in enumerate(loop_parts(t)):
+            send(t, LA + i, slot(x, z), part, node(x + way + 4, z))
+
+    def share(t):
+        send(t, SB, slot(x, z), (), sibling)
+
+    def ring_on(t):
         below, above = slot(x, z + 3), slot(x, z + 1)
         take(t, ZP, below, (0,))
         send(t, ZA, below, (0,), node(x, z + 1), z != 2)
         take(t, ZM + 1, above, (1,))
         send(t, ZB, above, (1,), node(x, z + 3), z != 1)
+
+    def ring_rest(t):
+        below, above = slot(x, z + 3), slot(x, z + 1)
         take(t, ZP + 1, below, (1,), z != 0)
         take(t, ZM, above, (0,), z != 3)
         side = z // 3
-        send(
-            t,
-            ZC,
-            slot(x, z + 1 + 2 * side),
-            (side,),
-            node(x, z + 3 + 2 * side),
-            outer,
-        )
+        send(t, ZC, slot(x, z + 1 + 2 * side), (side,), node(x, z + 3 + 2 * side), outer)
         send(t, XE, slot(x, 3 - z), (side,), node(x + away + 4, z), outer & gives)
         send(t, SB + 1, below, (), sibling, z != 0)
         send(t, SB + 2, above, (), sibling, z != 3)
 
-    def loop_hop(t):
-        for i, part in enumerate(loop_parts):
-            block = slot(x - loop_way[i] + 4, z)
-            take(t, LA + i, block, part)
-            send(t, LB + i, block, part, node(x + loop_way[i] + 4, z))
+    def loop_on(t, which):
+        for i, (part, way) in enumerate(loop_parts(t)):
+            if i in which:
+                block = slot(x - way + 4, z)
+                take(t, LA + i, block, part)
+                send(t, LB + i, block, part, node(x + way + 4, z))
 
     def cross(t):
         far = slot(x, z + 2)
@@ -240,8 +265,8 @@
 
     def settle(t):
         other = 1 - core
-        for i in range(len(loop_parts)):
-            take(t, LB + i, slot(x + 2, z), loop_parts[i])
+        for i, (part, _) in enumerate(loop_parts(t)):
+            take(t, LB + i, slot(x + 2, z), part)
         take(t, SB, slot(x, z, other), ())
         take(t, SB + 1, slot(x, z + 3, other), (), z != 0)
         take(t, SB + 2, slot(x, z + 1, other), (), z != 3)
@@ -263,7 +288,7 @@
         parts = [pools[t][block, s] for t in chunks]
         return parts[0] if len(parts) == 1 else jnp.concatenate(parts, axis=0)
 
-    def correlate(g):
+    def correlate(g, low, high):
         group = GROUPS[g]
         new, old, shapes = regions(group)
         earlier = tuple(range(group[0]))
@@ -271,15 +296,16 @@
         def product(first, second, chunks, sign):
             total = None
             for s in range(SEG):
-                for i, t in enumerate(group):
+                for t in group:
                     block = pools[t][first, s]
                     for m, turned in enumerate(rotate(block, sign)):
-                        at = m * new + i * CHUNK
+                        at = m * new + STARTS[t] - old
+                        end = at + SIZES[t]
                         if turned is None:
-                            rot[s, at : at + CHUNK] = block
+                            rot[s, at:end] = block
                         else:
-                            rot[s, at : at + CHUNK, :NF] = turned[0].astype(BF16)
-                            rot[s, at : at + CHUNK, NF:] = turned[1].astype(BF16)
+                            rot[s, at:end, :NF] = turned[0].astype(BF16)
+                            rot[s, at:end, NF:] = turned[1].astype(BF16)
                 term = lax.dot_general(
                     rot[s, : NLAG * new],
                     gather_rows(second, s, chunks),
@@ -290,7 +316,7 @@
             return total
 
         def one_pair(p, carry):
-            first, second = pairs[p, 0], pairs[p, 1]
+            first, second = pairs[0, p], pairs[1, p]
             todo = [(first, second, earlier + group, 1.0)]
             if old:
                 todo.append((second, first, earlier, -1.0))
@@ -305,7 +331,13 @@
                     across(g, r, d, p).start()
             return carry
 
-        lax.fori_loop(0, PAIRS, one_pair, 0)
+        run(one_pair, low, high)
+
+    def run(body, low, high):
+        if high - low == 1:
+            body(low, 0)
+        else:
+            lax.fori_loop(low, high, body, 0)
 
     def across(g, r, d, p):
         place = sum(spans[:g]) + r
@@ -319,92 +351,91 @@
             device_id_type=MESH,
         )
 
+    def store(p):
+        sem = in_sem.at[CHUNKS + TABLE_CUTS + 2 + p]
+        return pltpu.make_async_copy(out.at[p], result.at[0, p], sem)
+
     def finish(g):
         new, old, shapes = regions(GROUPS[g])
         scale = 1.0 / math.sqrt(NF * SEG * 4)
 
         def one_pair(p, carry):
-            for r in range(len(shapes)):
+            for r in range(spans[g]):
                 total = sends[g][r][y, p].astype(F32)
-                for d in (1, 2, 3):
+                for d in (1, 3, 2):
                     across(g, r, d, p).wait_recv()
                     total += lands[g][r][d - 1, p].astype(F32)
                 total *= scale
                 if r == 0:
-                    out[0, p, old : old + new, : old + new] = total[:, : old + new]
+                    out[p, old : old + new, : old + new] = total[:, : old + new]
                 else:
-                    out[0, p, :old, old : old + new] = total.T[:old]
-            return carry
-
-        lax.fori_loop(0, PAIRS, one_pair, 0)
-
-    spectra(0)
-    pl.semaphore_wait(barrier, len(partners))
-    first_hop(0)
-    spectra(1)
-    first_hop(1)
-    spectra(2)
-    spectra(3)
-    second_hop(0)
-    loop_hop(0)
-    first_hop(2)
-    cross(0)
-    second_hop(1)
-    loop_hop(1)
-    first_hop(3)
-    cross(1)
-    crossed(0)
-    second_hop(2)
-    loop_hop(2)
-    last_hop(0)
-    settle(0)
-    cross(2)
-    crossed(1)
-    second_hop(3)
-    loop_hop(3)
-    last_hop(1)
-    settle(1)
-    cross(3)
-    correlate(0)
-    crossed(2)
-    last_hop(2)
-    settle(2)
-    crossed(3)
-    correlate(1)
-    last_hop(3)
-    settle(3)
-    correlate(2)
-    for g in range(len(GROUPS)):
-        finish(g)
-    for done in started:
-        done()
-
-    def sent(p, carry):
-        for g in range(len(GROUPS)):
-            for r in range(spans[g]):
+                    out[p, :old, old : old + new] = total.T[:old]
                 for d in (1, 2, 3):
                     across(g, r, d, p).wait_send()
-        return carry
-
-    lax.fori_loop(0, PAIRS, sent, 0)
+            if g == len(GROUPS) - 1:
+                store(p).start()
+            return carry
+
+        lax.fori_loop(0, PAIRS, one_pair, 0)
+
+    steps = {
+        "S": spectra,
+        "Z": ring,
+        "O": loop,
+        "B": share,
+        "H": ring_on,
+        "I": ring_rest,
+        "L": lambda t: loop_on(t, (0, 1)),
+        "M": lambda t: loop_on(t, (2, 3)),
+        "X": cross,
+        "C": crossed,
+        "E": last_hop,
+        "T": settle,
+        "G": finish,
+    }
+    at = 0
+    while at < len(ORDER):
+        step = ORDER[at]
+        at += 1
+        if step[0] == "K":
+            g, low = int(step[1]), int(step[2])
+            high = low + 1
+            while at < len(ORDER) and ORDER[at] == step[:2] + str(high):
+                high += 1
+                at += 1
+            correlate(g, low, high)
+            step = "K" + str(g) + str(high - 1)
+        else:
+            steps[step[0]](int(step[1]))
+        if step == LAST:
+            for done in started:
+                done()
+        if step == "S0":
+            pl.semaphore_wait(barrier, len(partners))
+
+    for p in range(PAIRS):
+        store(p).wait()
 
 
 def local(traces, pairs):
     table, window, small = host_tables()
-    scratch = [pltpu.VMEM((BLOCKS, SEG, CHUNK, 2 * NF), BF16) for _ in range(CHUNKS)]
+    scratch = [pltpu.VMEM((BLOCKS, SEG, size, 2 * NF), BF16) for size in SIZES]
     spans = 0
     for group in GROUPS:
         shapes = regions(group)[2]
         spans += len(shapes)
         scratch += [pltpu.VMEM((NLAG, PAIRS, *shape), BF16) for shape in shapes]
         scratch += [pltpu.VMEM((3, PAIRS, *shape), BF16) for shape in shapes]
-    widest = max(len(group) for group in GROUPS) * CHUNK
+    widest = max(regions(group)[0] for group in GROUPS)
     scratch += [
         pltpu.VMEM((CB, SEG, L), BF16),
         pltpu.VMEM((L, 2 * NF), BF16),
-        pltpu.VMEM((2 * NF // 128, SEG * CHUNK, 128), F32),
+        pltpu.VMEM((NF, NF), BF16),
+        pltpu.VMEM((8, NF), F32),
+        pltpu.VMEM((2 * NF // 128, SEG * max(SIZES), 128), F32),
         pltpu.VMEM((SEG, NLAG * widest, 2 * NF), BF16),
-        pltpu.SemaphoreType.DMA((CHUNKS + TABLE_CUTS,)),
+        pltpu.VMEM((PAIRS, CB, CB), F32),
+        pltpu.SemaphoreType.DMA((CHUNKS + TABLE_CUTS + 2 + PAIRS,)),
         pltpu.SemaphoreType.DMA((CHUNKS, COPIES)),
         pltpu.SemaphoreType.DMA((CHUNKS, COPIES)),
         pltpu.SemaphoreType.DMA((spans, 3, PAIRS)),
@@ -416,17 +447,17 @@
         in_specs=[
             pl.BlockSpec(memory_space=pl.ANY),
             pl.BlockSpec(memory_space=pl.ANY),
-            pl.BlockSpec(memory_space=pltpu.VMEM),
-            pl.BlockSpec(memory_space=pltpu.VMEM),
+            pl.BlockSpec(memory_space=pl.ANY),
+            pl.BlockSpec(memory_space=pl.ANY),
             pl.BlockSpec(memory_space=pltpu.SMEM),
         ],
-        out_specs=pl.BlockSpec(memory_space=pltpu.VMEM),
+        out_specs=pl.BlockSpec(memory_space=pl.ANY),
         scratch_shapes=scratch,
         compiler_params=pltpu.CompilerParams(
             collective_id=0, has_side_effects=True, vmem_limit_bytes=62 << 20
         ),
         name="correlate_pairs",
-    )(traces, jnp.asarray(table), jnp.asarray(window), jnp.asarray(small), pairs)
+    )(traces, jnp.asarray(table), jnp.asarray(window), jnp.asarray(small), pairs.T)
 
 
 def solution(mesh):

time: 88.3 us -> 83.4 us (0.945)
  Pallas kernels: 84.2 us -> 80 us
  local copies, waits for them, and re-layouts: 3.62 us -> 2.29 us
    pallas_call x1, Pallas kernels: 84.2 us -> 80 us  [local(): pl.pallas_call(kernel, out_shape=jax.ShapeDtypeStruct((1, PAIRS, CB, CB),...]
    unnamed x2 -> x1, local copies, waits for them, and re-layouts: 3.62 us -> 2.29 us
where the time goes in v2:
time: 83.4 us; the launch traced here: 82.3 us
  Pallas kernels  80 us (96%)
  local copies, waits for them, and re-layouts  2.29 us (3%)
    pallas_call x1, Pallas kernels, local(): pl.pallas_call(kernel, out_shape=jax.ShapeDtypeStruct((1, PAIRS, CB, CB),...  80 us
    unnamed x1, local copies, waits for them, and re-layouts  2.29 us

profile of v2, /device:TPU:3, one launch (start us, length us, event | category | flops | bytes accessed | tf_op | source)
XLA Modules:
  0.0 82.3 jit_solution(16851531255721915055)
XLA Ops:
  0.0 80.0 %correlate_pairs.1 = f32[1,4,256,256]{3,2,1,0:T(8,128)} custom-call(bf16[256,2,4096]{2,1,0:T(2,128)(2,1)} %traces.1, bf16[4096,1024]{1,0:T(8,128)(2,1)} %constant.6.clone.table_hbm, bf16[512,512]{1,0:T(8,128)(2,1)} %constant.7.clone.window_hbm, f32[8,512]{1,0:T(8,128)} %constant.8.clone.small_hbm, s32[2,4]{1,0:T(2,128)} %bitcast.1), custom_call_target="tpu_custom_call" | custom-call | tf_op jit(solution)/shard_map/correlate_pairs/pallas_call | solution.py:444
  80.0 2.3 %copy.7 = f32[1,4,256,256]{3,2,1,0:T(8,128)} copy(f32[1,4,256,256]{3,2,1,0:T(8,128)} %correlate_pairs.1) | data formatting | bytes 2097152

commit v3 on v2

--- a/solution.py
+++ b/solution.py
@@ -29,11 +29,11 @@
 F32 = jnp.float32
 
 ORDER = (
-    "S0", "Z0", "O0", "S1", "S2", "S3", "Z1", "O2", "O1", "O3", "B1", "M0", "B0", "H0", "I0",
-    "M2", "H1", "I1", "X0", "L0", "Z2", "X1", "C0", "B3", "H2", "B2", "I2", "L1", "Z3", "E0",
-    "T0", "M1", "X2", "C1", "H3", "L2", "I3", "E1", "T1", "K00", "K01", "K02", "K03", "X3", "C2",
-    "L3", "E2", "T2", "K10", "K11", "K12", "K13", "M3", "C3", "E3", "T3", "K20", "K21", "K22",
-    "K23", "G0", "G1", "G2",
+    "S0", "Z0", "O0", "S1", "B1", "S2", "S3", "O2", "M0", "Z1", "O3", "B2", "O1", "H0", "I0",
+    "M2", "L0", "H1", "I1", "X0", "Z2", "X1", "M1", "C0", "H2", "I2", "L1", "B3", "Z3", "X2",
+    "B0", "E0", "T0", "C1", "L2", "H3", "I3", "E1", "T1", "K00", "K01", "K02", "C2", "E2", "K03",
+    "X3", "L3", "T2", "K10", "K11", "G0", "K12", "K13", "M3", "C3", "E3", "T3", "K20", "K21",
+    "K22", "K23", "G1", "G2",
 )
 
 LAST = "K" + str(len(GROUPS) - 1) + str(PAIRS - 1)

time: 83.4 us -> 82.8 us (level); the launches traced: 82.3 us -> 82.6 us
  no operation moved by 1% of the time
where the time goes in v3:
time: 82.8 us; the launch traced here: 82.6 us
  Pallas kernels  80.3 us (97%)
  local copies, waits for them, and re-layouts  2.29 us (3%)
    pallas_call x1, Pallas kernels, local(): pl.pallas_call(kernel, out_shape=jax.ShapeDtypeStruct((1, PAIRS, CB, CB),...  80.3 us
    unnamed x1, local copies, waits for them, and re-layouts  2.29 us

profile of v3, /device:TPU:3, one launch (start us, length us, event | category | flops | bytes accessed | tf_op | source)
XLA Modules:
  0.0 82.6 jit_solution(3810109427961775488)
XLA Ops:
  0.0 80.3 %correlate_pairs.1 = f32[1,4,256,256]{3,2,1,0:T(8,128)} custom-call(bf16[256,2,4096]{2,1,0:T(2,128)(2,1)} %traces.1, bf16[4096,1024]{1,0:T(8,128)(2,1)} %constant.6.clone.table_hbm, bf16[512,512]{1,0:T(8,128)(2,1)} %constant.7.clone.window_hbm, f32[8,512]{1,0:T(8,128)} %constant.8.clone.small_hbm, s32[2,4]{1,0:T(2,128)} %bitcast.1), custom_call_target="tpu_custom_call" | custom-call | tf_op jit(solution)/shard_map/correlate_pairs/pallas_call | solution.py:444
  80.3 2.3 %copy.7 = f32[1,4,256,256]{3,2,1,0:T(8,128)} copy(f32[1,4,256,256]{3,2,1,0:T(8,128)} %correlate_pairs.1) | data formatting | bytes 2097152

commit v4 on v3

--- a/solution.py
+++ b/solution.py
@@ -22,7 +22,7 @@
 CHUNKS = len(SIZES)
 STARTS = tuple(sum(SIZES[:t]) for t in range(CHUNKS))
 GROUPS = ((0, 1), (2,), (3,))
-TABLE_CUTS = 8
+TABLE_CUTS = 4
 AHEAD = 7
 MESH = pl.DeviceIdType.MESH
 BF16 = jnp.bfloat16

time: 82.8 us -> 82.8 us (level)
  no operation moved by 1% of the time
where the time goes in v4:
time: 82.8 us; the launch traced here: 82.7 us
  Pallas kernels  80.4 us (97%)
  local copies, waits for them, and re-layouts  2.29 us (3%)
    pallas_call x1, Pallas kernels, local(): pl.pallas_call(kernel, out_shape=jax.ShapeDtypeStruct((1, PAIRS, CB, CB),...  80.4 us
    unnamed x1, local copies, waits for them, and re-layouts  2.29 us

profile of v4, /device:TPU:3, one launch (start us, length us, event | category | flops | bytes accessed | tf_op | source)
XLA Modules:
  0.0 82.7 jit_solution(4241449887948821663)
XLA Ops:
  0.0 80.4 %correlate_pairs.1 = f32[1,4,256,256]{3,2,1,0:T(8,128)} custom-call(bf16[256,2,4096]{2,1,0:T(2,128)(2,1)} %traces.1, bf16[4096,1024]{1,0:T(8,128)(2,1)} %constant.6.clone.table_hbm, bf16[512,512]{1,0:T(8,128)(2,1)} %constant.7.clone.window_hbm, f32[8,512]{1,0:T(8,128)} %constant.8.clone.small_hbm, s32[2,4]{1,0:T(2,128)} %bitcast.1), custom_call_target="tpu_custom_call" | custom-call | tf_op jit(solution)/shard_map/correlate_pairs/pallas_call | solution.py:444
  80.4 2.3 %copy.7 = f32[1,4,256,256]{3,2,1,0:T(8,128)} copy(f32[1,4,256,256]{3,2,1,0:T(8,128)} %correlate_pairs.1) | data formatting | bytes 2097152
